TPU v7x, 32 devices: a whole 2x2x4 slice. The times are simulated.
32 devices in a mesh: band: 8 (over z, y), slab: 4 (over x, core).
Axes of the slice: x: 2, y: 2, z: 4, core: 2. Of those that a mesh axis runs over, the one named last changes fastest.
Arguments:
- bands: float32 [32, 32, 24, 128], P('band', 'slab'), may hold values from -8 to 8
- potential: float32 [32, 24, 128], P('slab'), may hold values from -1 to 0
Outputs:
- filtered: float32 [32, 32, 24, 128], P('band', 'slab')
- correlation: float32 [32, 32], P('band')
- projected: float32 [32, 32], P('band')
All inputs are finite; a program needn't handle non-finite values.
Results may differ from a plain program's by a relative error of at most 0.000092.
Values sent between devices are 32-bit elements; how exact they have to be, the bound alone decides.
A program may use at most 128 MiB of HBM per device.

v0:
```python
import functools

import jax
import jax.numpy as jnp
from jax import lax
from jax.experimental import pallas as pl
from jax.experimental.pallas import tpu as pltpu
from jax.sharding import PartitionSpec as P

centre = 4.5
half = 3.5
MESH = pl.DeviceIdType.MESH
STEPS = 4
BELOW, ABOVE = 4, 6


def shifted(v, axis):
    n = v.shape[axis]
    near = pltpu.roll(v, 1, axis) + pltpu.roll(v, n - 1, axis)
    far = pltpu.roll(v, 2, axis) + pltpu.roll(v, n - 2, axis)
    return near, far


def kernel(
    dims, bands, pot, f_out, c_out, p_out,
    e, vbuf, vt, turned, tails, blocks, ends, left, part, rb, rs,
    halo_send, halo_recv, load_sem, out_sem,
    block_send, block_recv, end_send, end_recv,
    row_send, row_recv, slab_send, slab_recv,
):
    nb, ns, L, nz, ny, nx, chunk, active, count, volume = dims
    J = count // 128
    b, s = lax.axis_index("band"), lax.axis_index("slab")
    up, down = lax.rem(s + 1, ns), lax.rem(s + ns - 1, ns)
    inner = pl.ds(BELOW * ny, nz * ny)
    base = BELOW * ny

    load = pltpu.make_async_copy(bands, e.at[0, :, inner], load_sem.at[0])
    load.start()
    load_pot = pltpu.make_async_copy(pot, vbuf.at[inner], load_sem.at[1])
    load_pot.start()

    barrier = pltpu.get_barrier_semaphore()

    def greet_band(d, carry):
        pl.semaphore_signal(
            barrier, inc=1, device_id={"band": lax.rem(b + d, nb)}, device_id_type=MESH
        )
        return carry

    lax.fori_loop(1, nb, greet_band, 0)
    for d in range(1, ns):
        pl.semaphore_signal(
            barrier, inc=1, device_id={"slab": lax.rem(s + d, ns)}, device_id_type=MESH
        )
    pl.semaphore_wait(barrier, nb - 1 + ns - 1)

    stale = base + (nz + 2) * ny
    if base + count > stale:
        spare = base + count - stale
        e[STEPS, :, stale:base + count, :] = jnp.zeros((L, spare, nx), jnp.float32)

    def pushed(src, dst, order, device):
        return pltpu.make_async_remote_copy(
            src_ref=src,
            dst_ref=dst,
            send_sem=halo_send.at[order],
            recv_sem=halo_recv.at[order],
            device_id={"slab": device},
            device_id_type=MESH,
        )

    def span(start, size):
        return pl.ds(start * ny, size * ny)

    def halo(stage, l):
        if stage == 0:
            low, high = bands.at[l, span(0, ABOVE)], bands.at[l, span(nz - BELOW, BELOW)]
        else:
            low, high = e.at[2, l, span(BELOW, ABOVE)], e.at[2, l, span(nz, BELOW)]
        k, order = 2 * stage, 2 * (stage * L + l)
        return (
            pushed(low, e.at[k, l, span(BELOW + nz, ABOVE)], order, down),
            pushed(high, e.at[k, l, span(0, BELOW)], order + 1, up),
        )

    def potential_halo():
        order = 4 * L
        low, high = pot.at[span(0, ABOVE - 2)], pot.at[span(nz - BELOW + 2, BELOW - 2)]
        return (
            pushed(low, vbuf.at[span(BELOW + nz, ABOVE - 2)], order, down),
            pushed(high, vbuf.at[span(2, BELOW - 2)], order + 1, up),
        )

    def plane(k, l, z):
        def rows(offset):
            start = (z + BELOW + offset) * ny
            return slice(start, start + ny)

        scale = (1.0 if k == 0 else 2.0) / half
        diagonal = (vbuf[rows(0), :] + (3.75 - centre)) * scale
        v = e[k, l, rows(0), :]
        near = e[k, l, rows(-1), :] + e[k, l, rows(1), :]
        far = e[k, l, rows(-2), :] + e[k, l, rows(2), :]
        for axis in (0, 1):
            n1, n2 = shifted(v, axis)
            near = near + n1
            far = far + n2
        value = diagonal * v - (scale * 2.0 / 3.0) * near + (scale / 24.0) * far
        if k > 0:
            value = value - e[k - 1, l, rows(0), :]
        e[k + 1, l, rows(0), :] = value

    def first_half(k, l):
        for z in range(2, nz - 2):
            plane(k, l, z)

    def second_half(k, l, stop):
        for z in (*range(-2, 2), *range(nz - 2, nz + 4)):
            plane(k, l, z)
        for z in range(stop):
            plane(k + 1, l, z)

    def send(src, dst, sent, arrived, peer):
        return pltpu.make_async_remote_copy(
            src_ref=src,
            dst_ref=dst,
            send_sem=sent,
            recv_sem=arrived,
            device_id={"band": peer},
            device_id_type=MESH,
        )

    def cells_of(peer):
        return pl.ds(pl.multiple_of(peer * chunk, 8), chunk)

    def block(l):
        return lambda d, peer: send(
            turned.at[:, l, cells_of(peer)], blocks.at[:, b, l],
            block_send.at[l, d], block_recv.at[l, d], peer,
        )

    def end(d, peer):
        return send(tails.at[peer], ends.at[:, b], end_send.at[d], end_recv.at[d], peer)

    def when_active(peer, action):
        if active == nb:
            action()
        else:
            pl.when(peer < active)(action)

    def each_peer(copies, action, everywhere=False):
        def step(d, carry):
            peer = lax.rem(b + d, nb)
            for copy in copies:
                if everywhere:
                    action(copy(d, peer))
                else:
                    when_active(peer, lambda copy=copy: action(copy(d, peer)))
            return carry

        lax.fori_loop(1, nb, step, 0)

    groups = [block(l) for l in range(L)] + [end]

    def turn(j, l):
        turned[j, l] = e[STEPS, l, base + 128 * j:base + 128 * (j + 1), :].T

    def correlate():
        own = cells_of(b)
        for j in range(J):
            blocks[j, b] = turned[j, :, own, :]
        ends[:, b] = tails[b]
        each_peer(groups, lambda copy: copy.wait_recv(), everywhere=True)
        flat = blocks.reshape(J * nb * L * chunk, 128)
        flat_ends = ends.reshape(J * nb * 2 * L, 128)

        def line(r):
            if r < chunk:
                pieces = [
                    flat[pl.ds(j * nb * L * chunk + r, nb * L, stride=chunk), :] for j in range(J)
                ]
            else:
                pieces = [
                    flat_ends[pl.ds(j * nb * 2 * L + r - chunk, nb * L, stride=2), :]
                    for j in range(J)
                ]
            return jnp.concatenate(pieces, axis=1)

        lane = lax.broadcasted_iota(jnp.int32, (nb * L, count), 1)
        y = lane
        for z in range(1, nz + 2):
            y = y - jnp.where(lane >= z * ny, ny, 0)
        inside_slab = lane < nz * ny
        mine = jnp.concatenate([vt[j, own, :] for j in range(J)], axis=1)

        def ahead(x, n):
            return pltpu.roll(x, count - n, 1)

        def split(x):
            high = x.astype(jnp.bfloat16)
            return high, (x - high.astype(jnp.float32)).astype(jnp.bfloat16)

        N = nb * L
        lines = [line(0), line(1)]
        for r in range(chunk):
            lines.append(line(r + 2))
            x = lines[r]
            near = lines[r + 1] + ahead(x, ny)
            near = near + jnp.where(y < ny - 1, ahead(x, 1), pltpu.roll(x, ny - 1, 1))
            far = lines[r + 2] + ahead(x, 2 * ny)
            far = far + jnp.where(y < ny - 2, ahead(x, 2), pltpu.roll(x, ny - 2, 1))
            w = (0.5 * mine[r:r + 1, :] + 1.875) * x - (2.0 / 3.0) * near + (1.0 / 24.0) * far
            x = jnp.where(inside_slab, x, 0.0)
            w = jnp.where(inside_slab, w, 0.0)
            place = pl.ds(r * count, count)
            xh, xl = split(x)
            wh, wl = split(w)
            for i, piece in enumerate((xh, xl, wh, wl)):
                left[i * N:(i + 1) * N, place] = piece
        out = sum(
            lax.dot_general(
                left[...], left[i * N:(i + 1) * N, :], (((1,), (1,)), ((), ())),
                preferred_element_type=jnp.float32,
            )
            for i in (1, 0)
        ) * volume
        gram = out[N:2 * N] + out[:N]
        skew = out[3 * N:] + out[2 * N:3 * N]
        proj = skew + skew.T
        for g in range(nb):
            part[g, 0:L, :] = gram[g * L:(g + 1) * L]
            part[g, L:2 * L, :] = proj[g * L:(g + 1) * L]

    def start(stage, l):
        for copy in halo(stage, l):
            copy.start()

    def arrive(stage, l):
        for copy in halo(stage, l):
            copy.wait_recv()

    def finish_band(l):
        first_half(2, l)
        arrive(1, l)
        second_half(2, l, nz + 2)
        for j in range(J):
            turn(j, l)
        each_peer([block(l)], lambda copy: copy.start())

    for copy in potential_halo():
        copy.start()
    for l in range(min(2, L)):
        start(0, l)
    load.wait()
    load_pot.wait()
    for l in range(L):
        first_half(0, l)
    for copy in potential_halo():
        copy.wait_recv()
    for l in range(L):
        arrive(0, l)
        second_half(0, l, nz)
        start(1, l)
        if l + 2 < L:
            start(0, l + 2)
        if l >= 1:
            finish_band(l - 1)
    finish_band(L - 1)
    for j in range(J):
        vt[j] = vbuf[base + 128 * j:base + 128 * (j + 1), :].T
    result = pltpu.make_async_copy(e.at[STEPS, :, inner], f_out, out_sem)
    result.start()
    for g in range(active):
        after = (g + 1) * chunk % nx
        for j in range(J):
            for l in range(L):
                tails[g, j, 2 * l:2 * l + 2, :] = turned[j, l, after:after + 2, :]
    each_peer([end], lambda copy: copy.start())
    if active == nb:
        correlate()
    else:
        pl.when(b < active)(correlate)

        @pl.when(b >= active)
        def _():
            part[...] = jnp.zeros_like(part)

    def row(d):
        peer = lax.rem(b + d, nb)
        return pltpu.make_async_remote_copy(
            src_ref=part.at[peer],
            dst_ref=rb.at[b],
            send_sem=row_send.at[d],
            recv_sem=row_recv.at[d],
            device_id={"band": peer},
            device_id_type=MESH,
        )

    def each_row(action):
        def step(d, carry):
            action(row(d))
            return carry

        lax.fori_loop(1, nb, step, 0)

    each_row(lambda copy: copy.start())
    rb[b] = part[b]
    each_row(lambda copy: copy.wait_recv())
    rs[s] = jnp.sum(rb[...], axis=0)

    def across(d):
        return pltpu.make_async_remote_copy(
            src_ref=rs.at[s],
            dst_ref=rs.at[s],
            send_sem=slab_send.at[d],
            recv_sem=slab_recv.at[d],
            device_id={"slab": lax.rem(s + d, ns)},
            device_id_type=MESH,
        )

    for d in range(1, ns):
        across(d).start()
    for d in range(1, ns):
        across(d).wait_recv()
    total = rs[0]
    for other in range(1, ns):
        total = total + rs[other]
    c_out[...] = total[:L]
    p_out[...] = total[L:]
    for d in range(1, ns):
        across(d).wait_send()
    each_row(lambda copy: copy.wait_send())
    for copy in potential_halo():
        copy.wait_send()
    for stage in (0, 1):
        for l in range(L):
            for copy in halo(stage, l):
                copy.wait_send()
    each_peer(groups, lambda copy: copy.wait_send())
    result.wait()


def body(bands, potential):
    L, nz, ny, nx = bands.shape
    nb, ns = lax.axis_size("band"), lax.axis_size("slab")
    rows = nz * ny
    tiles = nx // 8
    each = -(-tiles // nb)
    while tiles % each:
        each += 1
    chunk = each * 8
    active = nx // chunk
    count = -(-(nz + 2) * ny // 128) * 128
    J = count // 128
    held = max((nz + BELOW + ABOVE) * ny, BELOW * ny + count)
    dims = (nb, ns, L, nz, ny, nx, chunk, active, count, 1.0 / (rows * ns * nx))
    f32 = jnp.float32
    anywhere, vmem = pl.BlockSpec(memory_space=pl.ANY), pl.BlockSpec(memory_space=pltpu.VMEM)
    dma = pltpu.SemaphoreType.DMA
    f, c, p = pl.pallas_call(
        functools.partial(kernel, dims),
        out_shape=(
            pltpu.VMEM((L, rows, nx), f32),
            pltpu.VMEM((L, nb * L), f32),
            pltpu.VMEM((L, nb * L), f32),
        ),
        in_specs=[pl.BlockSpec(memory_space=pltpu.HBM)] * 2,
        out_specs=(anywhere, vmem, vmem),
        scratch_shapes=[
            pltpu.VMEM((STEPS + 1, L, held, nx), f32),
            pltpu.VMEM((held, nx), f32),
            pltpu.VMEM((J, nx, 128), f32),
            pltpu.VMEM((J, L, nx, 128), f32),
            pltpu.VMEM((nb, J, 2 * L, 128), f32),
            pltpu.VMEM((J, nb, L, chunk, 128), f32),
            pltpu.VMEM((J, nb, 2 * L, 128), f32),
            pltpu.VMEM((4 * nb * L, chunk * count), jnp.bfloat16),
            pltpu.VMEM((nb, 2 * L, nb * L), f32),
            pltpu.VMEM((nb, 2 * L, nb * L), f32),
            pltpu.VMEM((ns, 2 * L, nb * L), f32),
            dma((4 * L + 2,)), dma((4 * L + 2,)),
            dma((2,)), dma,
            dma((L, nb)), dma((L, nb)),
            dma((nb,)), dma((nb,)),
            dma((nb,)), dma((nb,)),
            dma((ns,)), dma((ns,)),
        ],
        compiler_params=pltpu.CompilerParams(
            collective_id=0, has_side_effects=True, vmem_limit_bytes=60 * 1024 * 1024
        ),
    )(bands.reshape(L, rows, nx), potential.reshape(rows, nx))
    return f.reshape(L, nz, ny, nx), c, p


def solution(mesh):
    in_specs = (P("band", "slab", None, None), P("slab", None, None))
    out_specs = (P("band", "slab", None, None), P("band", None), P("band", None))
    return jax.shard_map(body, mesh=mesh, in_specs=in_specs, out_specs=out_specs, check_vma=False)
```

profile of v0, /device:TPU:0, one launch (start us, length us, event | category | flops | bytes accessed | tf_op | source)
XLA Modules:
  0.0 40.8 jit_solution(10324306645487242558)
XLA Ops:
  0.6 38.3 %shard_map.49 = (f32[4,192,128]{2,1,0:T(8,128)S(1)}, f32[4,32]{1,0:T(4,128)S(1)}, f32[4,32]{1,0:T(4,128)S(1)}) custom-call(f32[4,192,128]{2,1,0:T(8,128)} %bitcast.4, f32[192,128]{1,0:T(8,128)} %bitcast.5), custom_call_target="tpu_custom_call" | custom-call | tf_op jit(solution)/shard_map/pallas_call | solution.py:361
  38.9 0.7 %copy.8 = f32[4,8,24,128]{3,2,1,0:T(8,128)} copy(f32[4,8,24,128]{3,2,1,0:T(8,128)S(1)} %bitcast.3) | data formatting | bytes 786432
  39.7 0.6 %copy.9 = f32[4,32]{1,0:T(4,128)} copy(f32[4,32]{1,0:T(4,128)S(1)} %get-tuple-element.10) | data formatting | bytes 1024
  40.3 0.6 %copy.10 = f32[4,32]{1,0:T(4,128)} copy(f32[4,32]{1,0:T(4,128)S(1)} %get-tuple-element.11) | data formatting | bytes 1024
where the time goes:
time: 41 us; the launch traced here: 40.8 us
  Pallas kernels  38.3 us (93%)
  local copies, waits for them, and re-layouts  1.9 us (5%)
  between operations  0.64 us (2%)
    pallas_call x1, Pallas kernels, body(): pl.pallas_call(functools.partial(kernel, dims), out_shape=(pltpu.VMEM((L,...  38.3 us
    unnamed x3, local copies, waits for them, and re-layouts  1.9 us

commit v1 on v0

--- a/solution.py
+++ b/solution.py
@@ -149,9 +149,18 @@
         else:
             pl.when(peer < active)(action)
 
+    def partner(d):
+        if nb & (nb - 1):
+            return lax.rem(b + d, nb)
+        peer, bit = 0, 1
+        while bit < nb:
+            peer = peer + lax.rem(lax.div(b, bit) + lax.div(nb - d, bit), 2) * bit
+            bit *= 2
+        return peer
+
     def each_peer(copies, action, everywhere=False):
         def step(d, carry):
-            peer = lax.rem(b + d, nb)
+            peer = partner(d)
             for copy in copies:
                 if everywhere:
                     action(copy(d, peer))
@@ -218,13 +227,11 @@
             wh, wl = split(w)
             for i, piece in enumerate((xh, xl, wh, wl)):
                 left[i * N:(i + 1) * N, place] = piece
-        out = sum(
-            lax.dot_general(
-                left[...], left[i * N:(i + 1) * N, :], (((1,), (1,)), ((), ())),
-                preferred_element_type=jnp.float32,
-            )
-            for i in (1, 0)
-        ) * volume
+        out = lax.dot_general(
+            left[...], left[0:2 * N, :], (((1,), (1,)), ((), ())),
+            preferred_element_type=jnp.float32,
+        )
+        out = (out[:, N:] + out[:, :N]) * volume
         gram = out[N:2 * N] + out[:N]
         skew = out[3 * N:] + out[2 * N:3 * N]
         proj = skew + skew.T

time: 41 us -> 40.7 us (level)
  no operation moved by 1% of the time
where the time goes in v1:
time: 40.7 us; the launch traced here: 40.5 us
  Pallas kernels  38 us (93%)
  local copies, waits for them, and re-layouts  1.9 us (5%)
  between operations  0.64 us (2%)
    pallas_call x1, Pallas kernels, body(): pl.pallas_call(functools.partial(kernel, dims), out_shape=(pltpu.VMEM((L,...  38 us
    unnamed x3, local copies, waits for them, and re-layouts  1.9 us

profile of v1, /device:TPU:0, one launch (start us, length us, event | category | flops | bytes accessed | tf_op | source)
XLA Modules:
  0.0 40.5 jit_solution(16694601483584282515)
XLA Ops:
  0.6 38.0 %shard_map.49 = (f32[4,192,128]{2,1,0:T(8,128)S(1)}, f32[4,32]{1,0:T(4,128)S(1)}, f32[4,32]{1,0:T(4,128)S(1)}) custom-call(f32[4,192,128]{2,1,0:T(8,128)} %bitcast.4, f32[192,128]{1,0:T(8,128)} %bitcast.5), custom_call_target="tpu_custom_call" | custom-call | tf_op jit(solution)/shard_map/pallas_call | solution.py:368
  38.6 0.7 %copy.8 = f32[4,8,24,128]{3,2,1,0:T(8,128)} copy(f32[4,8,24,128]{3,2,1,0:T(8,128)S(1)} %bitcast.3) | data formatting | bytes 786432
  39.4 0.6 %copy.9 = f32[4,32]{1,0:T(4,128)} copy(f32[4,32]{1,0:T(4,128)S(1)} %get-tuple-element.10) | data formatting | bytes 1024
  39.9 0.6 %copy.10 = f32[4,32]{1,0:T(4,128)} copy(f32[4,32]{1,0:T(4,128)S(1)} %get-tuple-element.11) | data formatting | bytes 1024
